TPU v7x, 256 devices: a whole 4x4x8 slice. The times are simulated.
256 devices in a mesh: pairs: 32 (over x, y, core), tm: 8 (over z).
Axes of the slice: x: 4, y: 4, z: 8, core: 2. Of those that a mesh axis runs over, the one named last changes fastest.
Arguments:
- spectra: bfloat16 [2, 8, 1024, 4096], P(None, 'tm', 'pairs')
- pair_blocks: int32 [32, 4, 2], replicated, may hold values from 0 to 31, as said below
- block_count: int32 [32], replicated, may hold values from 1 to 4, as said below
Outputs:
- stacked: float32 [128, 128, 2048], P('pairs', None, 'tm')
Inputs may be any that keep to these rules, and one draw needn't show every extreme that they name: pair_blocks[p, k] names two different channel blocks; block j holds channels j * 128 to (j + 1) * 128 - 1. Owner p's pair blocks are its slots 0 to block_count[p] - 1; its later slots are empty and their rows of stacked are zero.
All inputs are finite; a program needn't handle non-finite values.
Results may differ from a plain program's by a relative error of at most 0.006.
Values may be sent and summed in bfloat16 or wider, within the bound.
No kernel may reach another device: no remote copies, remote signals or barrier semaphores. Data moves between devices by JAX's collectives and lax.ppermute only.
A program may use at most 128 MiB of HBM per device.

v0:
```python
import functools
import math

import jax
import jax.numpy as jnp
import ml_dtypes
import numpy as np
from jax import lax
from jax.experimental import pallas as pl
from jax.experimental.pallas import tpu as pltpu
from jax.sharding import PartitionSpec as P

C = 4096
CB = 128
NF = 1024
FIRST_BIN = 16
FFT_LEN = 8192
LAGS = 2048
SMOOTH = 32
MAXB = 4
HOURS = 8
OWNERS = 32
amp_floor = 0.2

CHIPS = OWNERS // 2
BINS = NF // OWNERS
CHIP_BINS = 2 * BINS
LAG_PART = LAGS // HOURS
RANK_CHIP = 28
RANK_PART = 48
ROWS_CHIP = 2 * RANK_CHIP
ROWS_PART = 2 * RANK_PART
STEP = 2.0 * math.pi / FFT_LEN


def slepian(points, half_width, count):
    n = np.arange(points, dtype=np.float64)
    tri = np.diag(((points - 1) / 2.0 - n) ** 2 * math.cos(2.0 * math.pi * half_width))
    off = n[1:] * (points - n[1:]) / 2.0
    tri = tri + np.diag(off, 1) + np.diag(off, -1)
    vectors = np.linalg.eigh(tri)[1][:, ::-1][:, :count]
    return vectors * np.where(vectors[points // 2] < 0, -1.0, 1.0)


def split_rounded(table):
    high = table.astype(ml_dtypes.bfloat16)
    low = (table - high.astype(np.float64)).astype(ml_dtypes.bfloat16)
    return high, low


def real_form(table):
    return np.block([[table.real, -table.imag], [table.imag, table.real]])


@functools.cache
def tables():
    chip_basis = slepian(CHIP_BINS, LAGS / 2 / FFT_LEN, RANK_CHIP)
    part_basis = slepian(NF, LAG_PART / 2 / FFT_LEN, RANK_PART)
    bins = np.arange(NF) - (NF - 1) / 2.0
    lags = np.arange(LAG_PART) - LAG_PART // 2
    mid_bin = FIRST_BIN + (NF - 1) / 2.0
    compress = np.kron(np.eye(2), chip_basis.T)
    parts = []
    for part in range(HOURS // 2):
        mid_lag = LAG_PART * part - (LAGS - LAG_PART) // 2
        turned = np.exp(1j * STEP * (bins + mid_bin) * mid_lag)[:, None] * part_basis
        turned = turned.reshape(CHIPS, CHIP_BINS, RANK_PART)
        blocks = [(chip_basis.T @ turned[chip]).T for chip in range(CHIPS)]
        parts.append(np.concatenate(blocks, axis=1))
    combine = np.concatenate([half for part in parts for half in (part.real, part.imag)], axis=0)
    waves = np.exp(1j * STEP * np.outer(lags, bins)) @ part_basis
    waves = waves * np.exp(1j * STEP * mid_bin * lags)[:, None] / math.sqrt(NF)
    expand = real_form(waves)
    row = np.arange(BINS)[:, None] + SMOOTH
    column = np.arange(BINS + 2 * SMOOTH)[None, :]
    window = (np.abs(row - column) <= SMOOTH).astype(ml_dtypes.bfloat16)
    turned = [window[:, -SMOOTH:], window[:, SMOOTH:-SMOOTH], window[:, :SMOOTH]]
    window = np.stack([window, np.concatenate(turned, axis=1)])
    halves = np.split(compress, 2 * CHIP_BINS // BINS, axis=1)
    by_core = []
    for core in range(2):
        own, twin = core, 1 - core
        ordered = [halves[own], halves[2 + own], halves[twin], halves[2 + twin]]
        by_core.append(np.concatenate(split_rounded(np.concatenate(ordered, axis=1)), axis=1))
    compress = np.stack(by_core)
    padded = np.zeros((2 * CB, 2 * LAG_PART), ml_dtypes.bfloat16)
    for index, half in enumerate(split_rounded(expand)):
        padded[index * CB : index * CB + ROWS_PART] = half.T
    expand = padded
    return window, compress, split_rounded(combine), expand


def magnitude_of(real, imag):
    real, imag = real.astype(jnp.float32), imag.astype(jnp.float32)
    return jnp.sqrt(real * real + imag * imag).astype(jnp.bfloat16)


def whiten(core, window, source, first, centre, second, white):
    chunk = 512
    weights = window[core]
    for start in range(0, C, chunk):
        lanes = slice(start, start + chunk)
        sizes = jnp.concatenate([first[:, lanes], centre[:, lanes], second[:, lanes]], axis=0)
        sums = jnp.dot(weights, sizes, preferred_element_type=jnp.float32)
        inverse = 1.0 / (sums * (1.0 / (2 * SMOOTH + 1)) + 1e-05)
        for part in range(2):
            value = source[part, :, lanes].astype(jnp.float32) * inverse
            white[part, :, lanes] = value.astype(jnp.bfloat16)


def cross_of(blocks, base, white):
    crossed = []
    for slot in range(MAXB):
        left = pl.ds(pl.multiple_of(blocks[base + 2 * slot] * CB, CB), CB)
        right = pl.ds(pl.multiple_of(blocks[base + 2 * slot + 1] * CB, CB), CB)
        left_re = white[0, :, left].astype(jnp.float32)
        left_im = white[1, :, left].astype(jnp.float32)
        right_re = white[0, :, right].astype(jnp.float32)
        right_im = white[1, :, right].astype(jnp.float32)
        real = left_re * right_re + left_im * right_im
        imag = left_im * right_re - left_re * right_im
        crossed.append(jnp.concatenate([real, imag], axis=0).astype(jnp.bfloat16))
    return jnp.concatenate(crossed, axis=1)


def own_kernel(blocks, branch, window, own, near, own_size, twin_size, out, white):
    core = blocks[CHIPS * 2 * MAXB]
    whiten(core, window, own, near, own_size, twin_size, white)
    for chip in range(CHIPS):
        out[chip] = cross_of(blocks, chip * 2 * MAXB, white)


def twin_kernel(
    blocks, window, compress, twin, own_size, twin_size, far, own_cross, out, white
):
    core = blocks[CHIPS * 2 * MAXB]
    whiten(core, window, twin, own_size, twin_size, far, white)
    weights = compress[core]
    for chip in range(CHIPS):
        twin_cross = cross_of(blocks, chip * 2 * MAXB, white)
        cross = jnp.concatenate([own_cross[chip], twin_cross] * 2, axis=0)
        packed = jnp.dot(weights, cross, preferred_element_type=jnp.float32)
        out[chip] = packed.astype(jnp.bfloat16)


def combine_kernel(high, low, packed, out):
    wide = out.shape[2]
    real = [packed[chip, :RANK_CHIP, :wide] for chip in range(CHIPS)]
    imag = [packed[chip, RANK_CHIP:, :wide] for chip in range(CHIPS)]
    value = jnp.concatenate([jnp.concatenate(real, axis=0), jnp.concatenate(imag, axis=0)], axis=1)
    total = jnp.dot(high[...], value, preferred_element_type=jnp.float32)
    total = total + jnp.dot(low[...], value, preferred_element_type=jnp.float32)
    for part in range(HOURS // 2):
        base = part * ROWS_PART
        real_rows = slice(base, base + RANK_PART)
        imag_rows = slice(base + RANK_PART, base + ROWS_PART)
        real_real, real_imag = total[real_rows, :wide], total[real_rows, wide:]
        imag_real, imag_imag = total[imag_rows, :wide], total[imag_rows, wide:]
        for where, sign in ((part, 1.0), (HOURS - 1 - part, -1.0)):
            both = [real_real - sign * imag_imag, real_imag + sign * imag_real]
            out[where] = jnp.concatenate(both, axis=0).astype(jnp.bfloat16)


def stack_kernel(live, expand, parts, out, result, sems):
    blank = jnp.zeros((CB - ROWS_PART, CB), jnp.bfloat16)
    copies = []
    for slot in range(MAXB):
        lanes = slice(slot * CB, (slot + 1) * CB)
        rows = []
        for hour in range(HOURS):
            part = jnp.concatenate([parts[hour, :, lanes], blank], axis=0).T
            rows.append(jnp.concatenate([part, part], axis=1))
        lagged = jnp.dot(
            jnp.concatenate(rows, axis=0), expand[...], preferred_element_type=jnp.float32
        )
        linear = mean_real = mean_imag = None
        for hour in range(HOURS):
            correlation = lagged[hour * CB : (hour + 1) * CB, :LAG_PART]
            quadrature = lagged[hour * CB : (hour + 1) * CB, LAG_PART:]
            power = correlation * correlation + quadrature * quadrature
            inverse = jnp.minimum(lax.rsqrt(power), 1.0 / amp_floor)
            unit_real = correlation * inverse
            unit_imag = quadrature * inverse
            if hour == 0:
                linear, mean_real, mean_imag = correlation, unit_real, unit_imag
            else:
                linear = linear + correlation
                mean_real = mean_real + unit_real
                mean_imag = mean_imag + unit_imag
        stacked = linear * (mean_real * mean_real + mean_imag * mean_imag) * (1.0 / HOURS**3)
        result[slot] = jnp.where(live[slot] > 0, stacked, jnp.zeros_like(stacked))
        copy = pltpu.make_async_copy(result.at[slot], out.at[slot], sems.at[slot])
        copy.start()
        copies.append(copy)
    for copy in copies:
        copy.wait()


def on_device(spectra, pair_blocks, block_count):
    owner = lax.axis_index("pairs")
    core = owner % 2
    window, compress, (high, low), expand = tables()
    spectra = spectra[:, 0]
    twins = [(i, i ^ 1) for i in range(OWNERS)]
    twin = lax.ppermute(spectra, "pairs", twins)
    own_size = magnitude_of(spectra[0], spectra[1])
    last = OWNERS - 1
    near_pairs = [(i, i + 1) for i in range(1, last, 2)] + [(i, i - 1) for i in range(2, last, 2)]
    near = lax.ppermute(own_size, "pairs", near_pairs)
    twin_size = magnitude_of(twin[0], twin[1])
    slots = lax.dynamic_index_in_dim(
        pair_blocks.reshape(CHIPS, 2, 2 * MAXB), core, 1, keepdims=False
    )
    slots = jnp.concatenate([slots.reshape(-1), core[None]])
    count = lax.dynamic_index_in_dim(block_count, owner, 0, keepdims=False)
    live = (lax.broadcasted_iota(jnp.int32, (MAXB, 1, LAG_PART), 0) < count).astype(jnp.float32)
    near, twin_size, slots, count, live = lax.optimization_barrier(
        (near, twin_size, slots, count, live)
    )
    far = lax.ppermute(near, "pairs", twins)
    branch = lax.clamp(jnp.int32(0), count - 1, jnp.int32(MAXB - 1))
    vmem = pl.BlockSpec(memory_space=pltpu.VMEM)
    smem = pl.BlockSpec(memory_space=pltpu.SMEM)
    limit = pltpu.CompilerParams(vmem_limit_bytes=32 * 2**20)
    high, low = lax.optimization_barrier((jnp.asarray(high), jnp.asarray(low)))
    white = pltpu.VMEM((2, BINS, C), jnp.bfloat16)
    own_cross = pl.pallas_call(
        own_kernel,
        out_shape=jax.ShapeDtypeStruct((CHIPS, 2 * BINS, MAXB * CB), jnp.bfloat16),
        in_specs=[smem] * 2 + [vmem] * 5,
        out_specs=vmem,
        scratch_shapes=[white],
        compiler_params=limit,
        name="own_cross",
    )(slots, branch[None], window, spectra, near, own_size, twin_size)
    packed = pl.pallas_call(
        twin_kernel,
        out_shape=jax.ShapeDtypeStruct((CHIPS, ROWS_CHIP, MAXB * CB), jnp.bfloat16),
        in_specs=[smem] + [vmem] * 7,
        out_specs=vmem,
        scratch_shapes=[white],
        compiler_params=limit,
        name="twin_cross",
    )(slots, window, compress, twin, own_size, twin_size, far, own_cross)
    groups = [list(range(0, OWNERS, 2)), list(range(1, OWNERS, 2))]
    packed = lax.all_to_all(packed, "pairs", 0, 0, axis_index_groups=groups, tiled=True)

    def with_live(live):
        def exchange(packed, high, low):
            parts = pl.pallas_call(
                combine_kernel,
                out_shape=jax.ShapeDtypeStruct((HOURS, ROWS_PART, live * CB), jnp.bfloat16),
                in_specs=[vmem] * 3,
                out_specs=vmem,
                compiler_params=limit,
                name=f"combine_{live}",
            )(high, low, packed)
            parts = lax.all_to_all(parts, "tm", 0, 0, tiled=True)
            return jnp.pad(parts, ((0, 0), (0, 0), (0, (MAXB - live) * CB)))

        return exchange

    branches = [with_live(live) for live in range(1, MAXB + 1)]
    parts = lax.switch(count - 1, branches, packed, high, low)
    return pl.pallas_call(
        stack_kernel,
        out_shape=jax.ShapeDtypeStruct((MAXB, CB, LAG_PART), jnp.float32),
        in_specs=[vmem] * 3,
        out_specs=pl.BlockSpec(memory_space=pl.ANY),
        scratch_shapes=[
            pltpu.VMEM((MAXB, CB, LAG_PART), jnp.float32),
            pltpu.SemaphoreType.DMA((MAXB,)),
        ],
        compiler_params=limit,
        name="stack",
    )(live, expand, parts)


def solution(mesh):
    return jax.shard_map(
        on_device,
        mesh=mesh,
        in_specs=(P(None, "tm", "pairs", None), P(), P()),
        out_specs=P("pairs", None, "tm"),
        check_vma=False,
    )
```

profile of v0, /device:TPU:8, one launch (start us, length us, event | category | flops | bytes accessed | tf_op | source)
XLA Modules:
  0.0 66.7 jit_solution(5493448637763761477)
XLA Ops:
  0.0 1.2 %fusion.own_size = bf16[32,4096]{1,0:T(8,128)(2,1)S(1)} fusion(bf16[2,1,32,4096]{3,2,1,0:T(8,128)(2,1)} %param.12), kind=kLoop, calls=%fused_computation.2 | loop fusion | flops 786432 | bytes 786432 | tf_op jit(solution)/shard_map/sqrt | solution.py:95
  1.3 4.2 %collective-permute-start = (bf16[32,4096]{1,0:T(8,128)(2,1)S(1)}, bf16[32,4096]{1,0:T(8,128)(2,1)S(1)}, u32[]{:S(2)}, u32[]{:S(2)}) collective-permute-start(bf16[32,4096]{1,0:T(8,128)(2,1)S(1)} %fusion.own_size), channel_id=1, source_target_pairs={{8,16},{24,32},{40,48},{56,64},{72,80},{88,96},{104,112},{120,128}... | collective-permute-start | bytes 786440 | tf_op jit(solution)/shard_map/ppermute | solution.py:209
  5.5 0.7 %copy-done.6 = s32[32,4,2]{0,2,1:T(2,128)S(1)} copy-done((s32[32,4,2]{0,2,1:T(2,128)S(1)}, s32[32,4,2]{0,2,1:T(2,128)}, u32[]{:S(2)}) %copy-start.6) | copy-done | bytes 1048
  6.2 0.1 reshape.30
  6.3 0.1 constant_dynamic-slice_fusion
  6.4 0.2 copy.10
  6.5 0.1 reshape.31
  6.6 0.2 copy-done.7
  6.8 0.6 dynamic_slice.9
  7.4 0.6 compare_convert_fusion
  8.1 0.0 copy-start.2
  8.1 0.2 fusion.1.twin_size
  8.3 1.2 %collective-permute-done.near = bf16[32,4096]{1,0:T(8,128)(2,1)S(1)} collective-permute-done((bf16[32,4096]{1,0:T(8,128)(2,1)S(1)}, bf16[32,4096]{1,0:T(8,128)(2,1)S(1)}, u32[]{:S(2)}, u32[]{:S(2)}) %collective-permute-start) | collective-permute-done | bytes 262176 | tf_op jit(solution)/shard_map/ppermute | solution.py:209
  9.5 0.1 iota.7.live
  9.6 0.1 collective-permute-start.2
  10.4 0.0 copy-start.3
  10.4 1.4 %own_cross.1 = bf16[16,64,512]{2,1,0:T(8,128)(2,1)S(1)} custom-call(s32[129]{0:T(256)S(1)} %pad_add_fusion.blocks, s32[1]{0:T(128)} %bitcast.5.branch, bf16[2,32,96]{2,1,0:T(8,128)(2,1)S(1)} %copy-done.2, bf16[2,32,4096]{2,1,0:T(8,128)(2,1)S(1)} %bitcast.13, bf16[32,4096]{1,0:T(8,128)(2,1)S(1)} %collective-permute-done.near, ...), custom_call_target="tpu_custom_call" | custom-call | tf_op jit(solution)/shard_map/own_cross/pallas_call | solution.py:227
  11.8 2.8 %twin_cross.1 = bf16[16,56,512]{2,1,0:T(8,128)(2,1)} custom-call(s32[129]{0:T(256)S(1)} %pad_add_fusion.blocks, bf16[2,32,96]{2,1,0:T(8,128)(2,1)S(1)} %copy-done.2, bf16[2,56,256]{2,1,0:T(8,128)(2,1)S(1)} %copy-done.3, bf16[2,32,4096]{2,1,0:T(8,128)(2,1)S(1)} %collective-permute-done.1.twin, bf16[32,4096]{1,0:T(8,128)(2,1)S(1)} %fusion.own_size, ...), custom_call_target="tpu_custom_call" | custom-call | tf_op jit(solution)/shard_map/twin_cross/pallas_call | solution.py:236
  14.7 9.3 %all-to-all-start.4 = ((bf16[16,56,512]{2,1,0:T(8,128)(2,1)}), bf16[16,56,512]{2,1,0:T(8,128)(2,1)S(1)}, u32[]{:S(2)}, u32[]{:S(2)}) async-start(bf16[16,56,512]{2,1,0:T(8,128)(2,1)} %twin_cross.1), calls=%async_computation.4 | async-start | bytes 1835008 | tf_op jit(solution)/shard_map/all_to_all | solution.py:246
  23.9 14.9 %all-to-all-done.4 = bf16[16,56,512]{2,1,0:T(8,128)(2,1)S(1)} async-done(((bf16[16,56,512]{2,1,0:T(8,128)(2,1)}), bf16[16,56,512]{2,1,0:T(8,128)(2,1)S(1)}, u32[]{:S(2)}, u32[]{:S(2)}) %all-to-all-start.4) | async-done | bytes 917536 | tf_op jit(solution)/shard_map/all_to_all | solution.py:246
  38.9 25.4 %conditional.1 = (bf16[8,96,512]{2,1,0:T(8,128)(2,1)S(1)}) conditional(s32[]{:T(128)} %clamp.4, (bf16[384,448]{1,0:T(8,128)(2,1)S(1)}, bf16[384,448]{1,0:T(8,128)(2,1)S(1)}, bf16[16,56,512]{2,1,0:T(8,128)(2,1)S(1)}) %tuple.30, (bf16[384,448]{1,0:T(8,128)(2,1)S(1)}, bf16[384,448]{1,0:T(8,128)(2,1)S(1)}, ...), branch_computations={%region_0.1_spmd, %region_1.2_spmd, %region_2.3_spmd, %region_3.4_... | conditional | bytes 2555914 | solution.py:264
  38.9 1.0 %combine_4.1 = bf16[8,96,512]{2,1,0:T(8,128)(2,1)S(1)} custom-call(bf16[384,448]{1,0:T(8,128)(2,1)S(1)} %get-tuple-element.43.high, bf16[384,448]{1,0:T(8,128)(2,1)S(1)} %get-tuple-element.44.low, bf16[16,56,512]{2,1,0:T(8,128)(2,1)S(1)} %get-tuple-element.45.packed), custom_call_target="tpu_custom_call" | custom-call | tf_op jit(solution)/shard_map/cond/branch_3_fun/combine_4/pallas_call | solution.py:250
  39.9 24.4 %all_to_all.24 = bf16[8,96,512]{2,1,0:T(8,128)(2,1)S(1)} all-to-all(bf16[8,96,512]{2,1,0:T(8,128)(2,1)S(1)} %combine_4.1), channel_id=1, replica_groups=mesh['pairs'=32,'tm'=8] {'tm'}, dimensions={0} | all-to-all | bytes 1572864 | tf_op jit(solution)/shard_map/cond/branch_3_fun/all_to_all | solution.py:258
  64.3 2.5 %stack.1 = f32[4,128,256]{2,1,0:T(8,128)} custom-call(f32[4,1,256]{2,1,0:T(1,128)S(1)} %iota.7.live, bf16[256,512]{1,0:T(8,128)(2,1)S(1)} %copy-done.1, bf16[8,96,512]{2,1,0:T(8,128)(2,1)S(1)} %get-tuple-element.60.parts), custom_call_target="tpu_custom_call" | custom-call | tf_op jit(solution)/shard_map/stack/pallas_call | solution.py:265
  (16 shorter events, 0.0 us)
Async XLA Ops:
  0.0 8.1 %collective-permute-start.1 = (bf16[2,32,4096]{2,1,0:T(8,128)(2,1)}, bf16[2,32,4096]{2,1,0:T(8,128)(2,1)S(1)}, u32[]{:S(2)}, u32[]{:S(2)}) collective-permute-start(bf16[2,32,4096]{2,1,0:T(8,128)(2,1)} %bitcast.12), channel_id=1, source_target_pairs={{0,8},{8,0},{16,24},{24,16},{32,40},{40,32},{48,56},{56,48},{64,72... | collective-permute-start | bytes 1572872 | tf_op jit(solution)/shard_map/ppermute | solution.py:205
  1.3 8.3 %collective-permute-start = (bf16[32,4096]{1,0:T(8,128)(2,1)S(1)}, bf16[32,4096]{1,0:T(8,128)(2,1)S(1)}, u32[]{:S(2)}, u32[]{:S(2)}) collective-permute-start(bf16[32,4096]{1,0:T(8,128)(2,1)S(1)} %fusion.own_size), channel_id=1, source_target_pairs={{8,16},{24,32},{40,48},{56,64},{72,80},{88,96},{104,112},{120,128}... | collective-permute-start | bytes 786440 | tf_op jit(solution)/shard_map/ppermute | solution.py:209
  5.5 0.7 %copy-start.6 = (s32[32,4,2]{0,2,1:T(2,128)S(1)}, s32[32,4,2]{0,2,1:T(2,128)}, u32[]{:S(2)}) copy-start(s32[32,4,2]{0,2,1:T(2,128)} %param.13) | copy-start | bytes 3076
  6.2 0.7 copy-start.7
  6.3 4.1 %copy-start = (bf16[2,1,32,4096]{3,2,1,0:T(8,128)(2,1)S(1)}, bf16[2,1,32,4096]{3,2,1,0:T(8,128)(2,1)}, u32[]{:S(2)}) copy-start(bf16[2,1,32,4096]{3,2,1,0:T(8,128)(2,1)} %param.12) | copy-start | bytes 1572868
  8.1 2.3 %copy-start.2 = (bf16[2,32,96]{2,1,0:T(8,128)(2,1)S(1)}, bf16[2,32,96]{2,1,0:T(8,128)(2,1)}, u32[]{:S(2)}) copy-start(bf16[2,32,96]{2,1,0:T(8,128)(2,1)} %constant.56.clone.window) | copy-start | bytes 36868
  9.6 2.2 %collective-permute-start.2 = (bf16[32,4096]{1,0:T(8,128)(2,1)S(1)}, bf16[32,4096]{1,0:T(8,128)(2,1)S(1)}, u32[]{:S(2)}, u32[]{:S(2)}) collective-permute-start(bf16[32,4096]{1,0:T(8,128)(2,1)S(1)} %collective-permute-done.near), channel_id=1, source_target_pairs={{0,8},{8,0},{16,24},{24,16},{32,40},{40,32},{48,56},{56,48},{64,72... | collective-permute-start | bytes 786440 | tf_op jit(solution)/shard_map/ppermute | solution.py:220
  10.4 1.5 %copy-start.3 = (bf16[2,56,256]{2,1,0:T(8,128)(2,1)S(1)}, bf16[2,56,256]{2,1,0:T(8,128)(2,1)}, u32[]{:S(2)}) copy-start(bf16[2,56,256]{2,1,0:T(8,128)(2,1)} %constant.57.clone.compress) | copy-start | bytes 172036
  14.7 24.2 %copy-start.4 = (bf16[384,448]{1,0:T(8,128)(2,1)S(1)}, bf16[384,448]{1,0:T(8,128)(2,1)}, u32[]{:S(2)}) copy-start(bf16[384,448]{1,0:T(8,128)(2,1)} %constant.55.clone) | copy-start | bytes 1032196
  14.7 24.2 %copy-start.5 = (bf16[384,448]{1,0:T(8,128)(2,1)S(1)}, bf16[384,448]{1,0:T(8,128)(2,1)}, u32[]{:S(2)}) copy-start(bf16[384,448]{1,0:T(8,128)(2,1)} %constant.54.clone) | copy-start | bytes 1032196
  14.7 24.2 %all-to-all-start.4 = ((bf16[16,56,512]{2,1,0:T(8,128)(2,1)}), bf16[16,56,512]{2,1,0:T(8,128)(2,1)S(1)}, u32[]{:S(2)}, u32[]{:S(2)}) async-start(bf16[16,56,512]{2,1,0:T(8,128)(2,1)} %twin_cross.1), calls=%async_computation.4 | async-start | bytes 1835008 | tf_op jit(solution)/shard_map/all_to_all | solution.py:246
  38.9 25.4 %copy-start.1 = (bf16[256,512]{1,0:T(8,128)(2,1)S(1)}, bf16[256,512]{1,0:T(8,128)(2,1)}, u32[]{:S(2)}) copy-start(bf16[256,512]{1,0:T(8,128)(2,1)} %constant.58.clone.expand) | copy-start | bytes 786436
where the time goes:
time: 67.2 us; the launch traced here: 66.7 us
  blocking collectives  24.4 us (36%)
  waiting for transfers between devices  16.1 us (24%)
  starting transfers between devices  13.6 us (20%)
  Pallas kernels  7.71 us (11%)
  other arithmetic  2.12 us (3%)
  local copies, waits for them, and re-layouts  1.99 us (3%)
  between operations  0.81 us (1%)
    all_to_all x1, blocking collectives, exchange(): parts = lax.all_to_all(parts, 'tm', 0, 0, tiled=True)  24.4 us
    all_to_all x1, waiting for transfers between devices, on_device(): lax.all_to_all(packed, 'pairs', 0, 0, axis_index_groups=groups, tiled=True)  14.9 us
    all_to_all x1, starting transfers between devices, on_device(): lax.all_to_all(packed, 'pairs', 0, 0, axis_index_groups=groups, tiled=True)  9.28 us
    ppermute x1, starting transfers between devices, on_device(): near = lax.ppermute(own_size, 'pairs', near_pairs)  4.21 us
    pallas_call x1, Pallas kernels, on_device(): pl.pallas_call(twin_kernel, out_shape=jax.ShapeDtypeStruct((CHIPS, ROWS_C...  2.81 us
    pallas_call x1, Pallas kernels, on_device(): pl.pallas_call(stack_kernel, out_shape=jax.ShapeDtypeStruct((MAXB, CB, LA...  2.49 us
    sqrt x2, other arithmetic, magnitude_of(): return jnp.sqrt(real * real + imag * imag).astype(jnp.bfloat16)  1.46 us
    pallas_call x1, Pallas kernels, on_device(): pl.pallas_call(own_kernel, out_shape=jax.ShapeDtypeStruct((CHIPS, 2 * BIN...  1.43 us
  transfers between devices with their start and end apart: 4, of which 2 were waited for; matrix products, arithmetic and copies ran while one was open for 5% of the time, Pallas kernels for 2%

commit v1 on v0

--- a/solution.py
+++ b/solution.py
@@ -123,7 +123,7 @@
     return jnp.concatenate(crossed, axis=1)
 
 
-def own_kernel(blocks, branch, window, own, near, own_size, twin_size, out, white):
+def own_kernel(blocks, most, count, window, own, near, own_size, twin_size, out, white):
     core = blocks[CHIPS * 2 * MAXB]
     whiten(core, window, own, near, own_size, twin_size, white)
     for chip in range(CHIPS):
@@ -214,11 +214,13 @@
     slots = jnp.concatenate([slots.reshape(-1), core[None]])
     count = lax.dynamic_index_in_dim(block_count, owner, 0, keepdims=False)
     live = (lax.broadcasted_iota(jnp.int32, (MAXB, 1, LAG_PART), 0) < count).astype(jnp.float32)
-    near, twin_size, slots, count, live = lax.optimization_barrier(
-        (near, twin_size, slots, count, live)
+    most = jnp.max(jnp.where(lax.iota(jnp.int32, OWNERS) % 2 == core, block_count, 0))
+    first, last_live = jnp.int32(0), jnp.int32(MAXB - 1)
+    branches = [lax.clamp(first, value - 1, last_live) for value in (most, count)]
+    near, twin_size, slots, live, *branches = lax.optimization_barrier(
+        (near, twin_size, slots, live, *branches)
     )
     far = lax.ppermute(near, "pairs", twins)
-    branch = lax.clamp(jnp.int32(0), count - 1, jnp.int32(MAXB - 1))
     vmem = pl.BlockSpec(memory_space=pltpu.VMEM)
     smem = pl.BlockSpec(memory_space=pltpu.SMEM)
     limit = pltpu.CompilerParams(vmem_limit_bytes=32 * 2**20)
@@ -227,12 +229,12 @@
     own_cross = pl.pallas_call(
         own_kernel,
         out_shape=jax.ShapeDtypeStruct((CHIPS, 2 * BINS, MAXB * CB), jnp.bfloat16),
-        in_specs=[smem] * 2 + [vmem] * 5,
+        in_specs=[smem] * 3 + [vmem] * 5,
         out_specs=vmem,
         scratch_shapes=[white],
         compiler_params=limit,
         name="own_cross",
-    )(slots, branch[None], window, spectra, near, own_size, twin_size)
+    )(slots, *(branch[None] for branch in branches), window, spectra, near, own_size, twin_size)
     packed = pl.pallas_call(
         twin_kernel,
         out_shape=jax.ShapeDtypeStruct((CHIPS, ROWS_CHIP, MAXB * CB), jnp.bfloat16),
@@ -243,7 +245,20 @@
         name="twin_cross",
     )(slots, window, compress, twin, own_size, twin_size, far, own_cross)
     groups = [list(range(0, OWNERS, 2)), list(range(1, OWNERS, 2))]
-    packed = lax.all_to_all(packed, "pairs", 0, 0, axis_index_groups=groups, tiled=True)
+
+    def widen(parts, slots):
+        return jnp.pad(parts, ((0, 0), (0, 0), (0, (MAXB - slots) * CB)))
+
+    def between_chips(slots):
+        def exchange(packed):
+            packed = lax.all_to_all(
+                packed[:, :, : slots * CB], "pairs", 0, 0, axis_index_groups=groups, tiled=True
+            )
+            return widen(packed, slots)
+
+        return exchange
+
+    packed = lax.switch(most - 1, [between_chips(slots) for slots in range(1, MAXB + 1)], packed)
 
     def with_live(live):
         def exchange(packed, high, low):
@@ -256,12 +271,13 @@
                 name=f"combine_{live}",
             )(high, low, packed)
             parts = lax.all_to_all(parts, "tm", 0, 0, tiled=True)
-            return jnp.pad(parts, ((0, 0), (0, 0), (0, (MAXB - live) * CB)))
+            return widen(parts, live)
 
         return exchange
 
-    branches = [with_live(live) for live in range(1, MAXB + 1)]
-    parts = lax.switch(count - 1, branches, packed, high, low)
+    parts = lax.switch(
+        count - 1, [with_live(live) for live in range(1, MAXB + 1)], packed, high, low
+    )
     return pl.pallas_call(
         stack_kernel,
         out_shape=jax.ShapeDtypeStruct((MAXB, CB, LAG_PART), jnp.float32),

time: 67.2 us -> 65.2 us (0.970)
  the two profiles are of different devices: /device:TPU:8 before, /device:TPU:24 now
where the time goes in v1:
time: 65.2 us; the launch traced here: 65.1 us
  blocking collectives  46.5 us (71%)
  Pallas kernels  6.64 us (10%)
  starting transfers between devices  5.38 us (8%)
  other arithmetic  2.81 us (4%)
  local copies, waits for them, and re-layouts  1.86 us (3%)
  between operations  1.47 us (2%)
    all_to_all x1, blocking collectives, exchange(): parts = lax.all_to_all(parts, 'tm', 0, 0, tiled=True)  26.2 us
    all_to_all x1, blocking collectives, exchange(): lax.all_to_all(packed[:, :, :slots * CB], 'pairs', 0, 0, axis_index_group...  20.4 us
    ppermute x1, starting transfers between devices, on_device(): near = lax.ppermute(own_size, 'pairs', near_pairs)  2.76 us
    ppermute x1, starting transfers between devices, on_device(): far = lax.ppermute(near, 'pairs', twins)  2.62 us
    pallas_call x1, Pallas kernels, on_device(): pl.pallas_call(stack_kernel, out_shape=jax.ShapeDtypeStruct((MAXB, CB, LA...  2.49 us
    pallas_call x1, Pallas kernels, on_device(): pl.pallas_call(twin_kernel, out_shape=jax.ShapeDtypeStruct((CHIPS, ROWS_C...  1.93 us
    sqrt x2, other arithmetic, magnitude_of(): return jnp.sqrt(real * real + imag * imag).astype(jnp.bfloat16)  1.46 us
    pallas_call x1, Pallas kernels, on_device(): pl.pallas_call(own_kernel, out_shape=jax.ShapeDtypeStruct((CHIPS, 2 * BIN...  1.43 us
  transfers between devices with their start and end apart: 3, of which 1 were waited for; matrix products, arithmetic and copies ran while one was open for 6% of the time, Pallas kernels for 2%

profile of v1, /device:TPU:24, one launch (start us, length us, event | category | flops | bytes accessed | tf_op | source)
XLA Modules:
  0.0 65.1 jit_solution(13178292788219077508)
XLA Ops:
  0.0 1.2 %fusion.own_size = bf16[32,4096]{1,0:T(8,128)(2,1)S(1)} fusion(bf16[2,1,32,4096]{3,2,1,0:T(8,128)(2,1)} %param.16), kind=kLoop, calls=%fused_computation.2 | loop fusion | flops 786432 | bytes 786432 | tf_op jit(solution)/shard_map/sqrt | solution.py:95
  1.3 2.8 %collective-permute-start = (bf16[32,4096]{1,0:T(8,128)(2,1)S(1)}, bf16[32,4096]{1,0:T(8,128)(2,1)S(1)}, u32[]{:S(2)}, u32[]{:S(2)}) collective-permute-start(bf16[32,4096]{1,0:T(8,128)(2,1)S(1)} %fusion.own_size), channel_id=1, source_target_pairs={{8,16},{24,32},{40,48},{56,64},{72,80},{88,96},{104,112},{120,128}... | collective-permute-start | bytes 786440 | tf_op jit(solution)/shard_map/ppermute | solution.py:209
  4.0 0.6 copy-done.7
  4.7 0.6 dynamic_slice.9
  5.3 0.7 %fusion.2 = s32[]{:T(128)} fusion(s32[32]{0:T(128)S(1)} %copy-done.7, s32[]{:T(128)} %select_n.25), kind=kLoop, calls=%fused_computation.8 | loop fusion | flops 287 | bytes 136 | tf_op jit(solution)/shard_map/reduce_max | solution.py:217
  7.3 0.0 copy-done.6
  7.3 0.1 reshape.30
  7.4 0.1 constant_dynamic-slice_fusion
  7.5 0.2 copy.10
  7.7 0.1 reshape.31
  7.8 0.7 %compare_convert_fusion = f32[4]{0:T(128)S(1)} fusion(s32[]{:T(128)} %bitcast.4), kind=kLoop, calls=%fused_computation.6 | loop fusion | flops 8 | bytes 20 | tf_op jit(solution)/shard_map/convert_element_type | solution.py:216
  8.5 0.2 fusion.1.twin_size
  8.7 0.3 collective-permute-done.near
  8.9 0.1 iota.10.live
  9.0 2.6 %collective-permute-start.2 = (bf16[32,4096]{1,0:T(8,128)(2,1)S(1)}, bf16[32,4096]{1,0:T(8,128)(2,1)S(1)}, u32[]{:S(2)}, u32[]{:S(2)}) collective-permute-start(bf16[32,4096]{1,0:T(8,128)(2,1)S(1)} %collective-permute-done.near), channel_id=1, source_target_pairs={{0,8},{8,0},{16,24},{24,16},{32,40},{40,32},{48,56},{56,48},{64,72... | collective-permute-start | bytes 786440 | tf_op jit(solution)/shard_map/ppermute | solution.py:223
  11.6 1.4 %own_cross.1 = bf16[16,64,512]{2,1,0:T(8,128)(2,1)S(1)} custom-call(s32[129]{0:T(256)S(1)} %pad_add_fusion.blocks, s32[1]{0:T(128)} %bitcast.5.most, s32[1]{0:T(128)} %bitcast.6.count, bf16[2,32,96]{2,1,0:T(8,128)(2,1)S(1)} %copy-done.2, bf16[2,32,4096]{2,1,0:T(8,128)(2,1)S(1)} %bitcast.14, bf16[32,4096]{1,0:T(8,128)(2,1)S(1)} %collective-permute-done.near, ...), custom_call_target="tpu_custom_call" | custom-call | tf_op jit(solution)/shard_map/own_cross/pallas_call | solution.py:229
  13.1 1.9 %twin_cross.1 = bf16[16,56,512]{2,1,0:T(8,128)(2,1)S(1)} custom-call(s32[129]{0:T(256)S(1)} %pad_add_fusion.blocks, bf16[2,32,96]{2,1,0:T(8,128)(2,1)S(1)} %copy-done.2, bf16[2,56,256]{2,1,0:T(8,128)(2,1)S(1)} %copy-done.3, bf16[2,32,4096]{2,1,0:T(8,128)(2,1)S(1)} %collective-permute-done.1.twin, bf16[32,4096]{1,0:T(8,128)(2,1)S(1)} %fusion.own_size, ...), custom_call_target="tpu_custom_call" | custom-call | tf_op jit(solution)/shard_map/twin_cross/pallas_call | solution.py:238
  15.1 20.4 %conditional.2 = (bf16[16,56,512]{2,1,0:T(8,128)(2,1)S(1)}) conditional(s32[]{:T(128)} %clamp.8, bf16[16,56,512]{2,1,0:T(8,128)(2,1)S(1)} %twin_cross.1, bf16[16,56,512]{2,1,0:T(8,128)(2,1)S(1)} %twin_cross.1, bf16[16,56,512]{2,1,0:T(8,128)(2,1)S(1)} %twin_cross.1, bf16[16,56,512]{2,1,0:T(8,128)(2,1)S(1)} %twin_cross.1), branch_computations={%region_1.2_spmd, %region_2.3_spmd, %region_3.4_spmd, %region_4.5_... | conditional | bytes 4358154 | solution.py:261
  15.1 20.4 %all_to_all.35 = bf16[16,56,512]{2,1,0:T(8,128)(2,1)S(1)} all-to-all(bf16[16,56,512]{2,1,0:T(8,128)(2,1)S(1)} %param.3), channel_id=1, replica_groups={{0,16,32,48,64,80,96,112,128,144,160,176,192,208,224,240},{8,24,40,56,7..., dimensions={0} | all-to-all | bytes 1835008 | tf_op jit(solution)/shard_map/cond/branch_3_fun/all_to_all | solution.py:254
  35.5 27.1 %conditional.3 = (bf16[8,96,512]{2,1,0:T(8,128)(2,1)S(1)}) conditional(s32[]{:T(128)} %clamp.9, (bf16[384,448]{1,0:T(8,128)(2,1)S(1)}, bf16[384,448]{1,0:T(8,128)(2,1)S(1)}, bf16[16,56,512]{2,1,0:T(8,128)(2,1)S(1)}) %tuple.46, (bf16[384,448]{1,0:T(8,128)(2,1)S(1)}, bf16[384,448]{1,0:T(8,128)(2,1)S(1)}, ...), branch_computations={%region_5.6_spmd, %region_6.7_spmd, %region_7.8_spmd, %region_8.9_... | conditional | bytes 2555914 | solution.py:278
  35.5 0.8 %combine_3.1 = bf16[8,96,384]{2,1,0:T(8,128)(2,1)S(1)} custom-call(bf16[384,448]{1,0:T(8,128)(2,1)S(1)} %get-tuple-element.49.high, bf16[384,448]{1,0:T(8,128)(2,1)S(1)} %get-tuple-element.50.low, bf16[16,56,512]{2,1,0:T(8,128)(2,1)S(1)} %get-tuple-element.51.packed), custom_call_target="tpu_custom_call" | custom-call | tf_op jit(solution)/shard_map/cond/branch_2_fun/combine_3/pallas_call | solution.py:265
  36.3 26.2 %all_to_all.38 = bf16[8,96,384]{2,1,0:T(8,128)(2,1)S(1)} all-to-all(bf16[8,96,384]{2,1,0:T(8,128)(2,1)S(1)} %combine_3.1), channel_id=1, replica_groups=mesh['pairs'=32,'tm'=8] {'tm'}, dimensions={0} | all-to-all | bytes 1179648 | tf_op jit(solution)/shard_map/cond/branch_2_fun/all_to_all | solution.py:273
  62.5 0.1 pad.23
  62.6 2.5 %stack.1 = f32[4,128,256]{2,1,0:T(8,128)} custom-call(f32[4,1,256]{2,1,0:T(1,128)S(1)} %iota.10.live, bf16[256,512]{1,0:T(8,128)(2,1)S(1)} %copy-done.1, bf16[8,96,512]{2,1,0:T(8,128)(2,1)S(1)} %get-tuple-element.72.parts), custom_call_target="tpu_custom_call" | custom-call | tf_op jit(solution)/shard_map/stack/pallas_call | solution.py:281
  (18 shorter events, 0.1 us)
Async XLA Ops:
  0.0 8.4 %collective-permute-start.1 = (bf16[2,32,4096]{2,1,0:T(8,128)(2,1)}, bf16[2,32,4096]{2,1,0:T(8,128)(2,1)S(1)}, u32[]{:S(2)}, u32[]{:S(2)}) collective-permute-start(bf16[2,32,4096]{2,1,0:T(8,128)(2,1)} %bitcast.13), channel_id=1, source_target_pairs={{0,8},{8,0},{16,24},{24,16},{32,40},{40,32},{48,56},{56,48},{64,72... | collective-permute-start | bytes 1572872 | tf_op jit(solution)/shard_map/ppermute | solution.py:205
  1.3 7.7 %collective-permute-start = (bf16[32,4096]{1,0:T(8,128)(2,1)S(1)}, bf16[32,4096]{1,0:T(8,128)(2,1)S(1)}, u32[]{:S(2)}, u32[]{:S(2)}) collective-permute-start(bf16[32,4096]{1,0:T(8,128)(2,1)S(1)} %fusion.own_size), channel_id=1, source_target_pairs={{8,16},{24,32},{40,48},{56,64},{72,80},{88,96},{104,112},{120,128}... | collective-permute-start | bytes 786440 | tf_op jit(solution)/shard_map/ppermute | solution.py:209
  4.0 0.7 %copy-start.7 = (s32[32]{0:T(128)S(1)}, s32[32]{0:T(128)}, u32[]{:S(2)}) copy-start(s32[32]{0:T(128)} %param.18) | copy-start | bytes 388
  6.6 0.7 %copy-start.6 = (s32[32,4,2]{0,2,1:T(2,128)S(1)}, s32[32,4,2]{0,2,1:T(2,128)}, u32[]{:S(2)}) copy-start(s32[32,4,2]{0,2,1:T(2,128)} %param.17) | copy-start | bytes 3076
  7.4 4.3 %copy-start = (bf16[2,1,32,4096]{3,2,1,0:T(8,128)(2,1)S(1)}, bf16[2,1,32,4096]{3,2,1,0:T(8,128)(2,1)}, u32[]{:S(2)}) copy-start(bf16[2,1,32,4096]{3,2,1,0:T(8,128)(2,1)} %param.16) | copy-start | bytes 1572868
  8.4 3.2 %copy-start.2 = (bf16[2,32,96]{2,1,0:T(8,128)(2,1)S(1)}, bf16[2,32,96]{2,1,0:T(8,128)(2,1)}, u32[]{:S(2)}) copy-start(bf16[2,32,96]{2,1,0:T(8,128)(2,1)} %constant.78.clone.window) | copy-start | bytes 36868
  9.0 4.1 %collective-permute-start.2 = (bf16[32,4096]{1,0:T(8,128)(2,1)S(1)}, bf16[32,4096]{1,0:T(8,128)(2,1)S(1)}, u32[]{:S(2)}, u32[]{:S(2)}) collective-permute-start(bf16[32,4096]{1,0:T(8,128)(2,1)S(1)} %collective-permute-done.near), channel_id=1, source_target_pairs={{0,8},{8,0},{16,24},{24,16},{32,40},{40,32},{48,56},{56,48},{64,72... | collective-permute-start | bytes 786440 | tf_op jit(solution)/shard_map/ppermute | solution.py:223
  11.6 1.5 %copy-start.3 = (bf16[2,56,256]{2,1,0:T(8,128)(2,1)S(1)}, bf16[2,56,256]{2,1,0:T(8,128)(2,1)}, u32[]{:S(2)}) copy-start(bf16[2,56,256]{2,1,0:T(8,128)(2,1)} %constant.79.clone.compress) | copy-start | bytes 172036
  15.0 20.4 %copy-start.4 = (bf16[384,448]{1,0:T(8,128)(2,1)S(1)}, bf16[384,448]{1,0:T(8,128)(2,1)}, u32[]{:S(2)}) copy-start(bf16[384,448]{1,0:T(8,128)(2,1)} %constant.77.clone) | copy-start | bytes 1032196
  15.1 20.4 %copy-start.5 = (bf16[384,448]{1,0:T(8,128)(2,1)S(1)}, bf16[384,448]{1,0:T(8,128)(2,1)}, u32[]{:S(2)}) copy-start(bf16[384,448]{1,0:T(8,128)(2,1)} %constant.76.clone) | copy-start | bytes 1032196
  35.5 27.1 %copy-start.1 = (bf16[256,512]{1,0:T(8,128)(2,1)S(1)}, bf16[256,512]{1,0:T(8,128)(2,1)}, u32[]{:S(2)}) copy-start(bf16[256,512]{1,0:T(8,128)(2,1)} %constant.80.clone.expand) | copy-start | bytes 786436
